TPU v7x, 32 devices: a whole 2x2x4 slice. The times are simulated.
32 devices in a mesh: dp: 8 (over y, x, core), mp: 4 (over z).
Axes of the slice: x: 2, y: 2, z: 4, core: 2. Of those that a mesh axis runs over, the one named last changes fastest.
Arguments:
- hidden: bfloat16 [2, 512, 4224], P(None, 'dp'), may hold values from 0 to 6, as said below
- proj_weight: bfloat16 [4224, 4224], P(None, 'mp'), may hold values from -0.09375 to 0.09375
Outputs:
- grad_first: bfloat16 [512, 4224], P('dp', 'mp')
Inputs may be any that keep to these rules, and one draw needn't show every extreme that they name: `hidden`: rectified features of 512 images in two views.
All inputs are finite; a program needn't handle non-finite values.
Results may differ from a plain program's by a relative error of at most 0.0057.
Values may be sent and summed in bfloat16 or wider, within the bound.
A program may use at most 64 MiB of HBM per device.

v0:
```python
import jax
import jax.numpy as jnp
from jax import lax
from jax.sharding import PartitionSpec as P

off_weight = 0.0051
eps = 1e-05


def shards(hidden, proj_weight):
    mp_index = lax.axis_index("mp")
    dp_index = lax.axis_index("dp")
    dp_count = lax.axis_size("dp")
    rows = proj_weight.shape[1]
    total = hidden.shape[1] * dp_count
    feats = jnp.einsum("vbh,hc->vbc", hidden, proj_weight, preferred_element_type=jnp.float32)
    sums = lax.psum(jnp.sum(feats, axis=1, keepdims=True), "dp")
    mean = sums / total
    centered = feats - mean
    var = lax.psum(jnp.sum(centered * centered, axis=1, keepdims=True), "dp") / total
    normed = (centered / jnp.sqrt(var + eps)).astype(jnp.bfloat16)
    inv_std = 1.0 / jnp.sqrt(var + eps)
    first = normed[0]
    second = normed[1]
    second_full = lax.all_gather(second, "mp", axis=1, tiled=True)
    width = second_full.shape[1] // dp_count
    columns = lax.all_to_all(second_full, "dp", split_axis=1, concat_axis=0, tiled=True)
    corr = (
        jnp.einsum(
            "bi,bj->ij",
            lax.all_gather(first, "dp", axis=0, tiled=True),
            columns,
            preferred_element_type=jnp.float32,
        )
        / total
    )
    row_ids = mp_index * rows + lax.iota(jnp.int32, rows)[:, None]
    col_ids = dp_index * width + lax.iota(jnp.int32, width)[None, :]
    grad_block = jnp.where(row_ids == col_ids, 2.0 * (corr - 1.0), 2.0 * off_weight * corr).astype(
        jnp.bfloat16
    )
    grad_rows = lax.all_gather(grad_block, "dp", axis=1, tiled=True)
    grad_wide = grad_rows.astype(jnp.float32)
    all_cols = lax.iota(jnp.int32, grad_rows.shape[1])[None, :]
    diag_val = jnp.sum(jnp.where(all_cols == row_ids, grad_wide, 0.0), axis=1)
    scale_sum = (jnp.sum(grad_wide * grad_wide, axis=1) - diag_val * diag_val) / (
        2.0 * off_weight
    ) + diag_val * (1.0 + diag_val / 2.0)
    back = jnp.einsum("bj,ij->bi", second_full, grad_rows, preferred_element_type=jnp.float32)
    result = (back - first.astype(jnp.float32) * scale_sum[None, :]) * inv_std[0]
    return result.astype(jnp.bfloat16)


def solution(mesh):
    return jax.shard_map(
        shards,
        mesh=mesh,
        in_specs=(P(None, "dp", None), P(None, "mp")),
        out_specs=P("dp", "mp"),
        check_vma=False,
    )
```

profile of v0, /device:TPU:0, one launch (start us, length us, event | category | flops | bytes accessed | tf_op | source)
XLA Modules:
  0.0 188.0 jit_solution(16482395339679156735)
XLA Ops:
  6.5 0.0 copy-start
  6.5 0.0 all-gather.7.cloned.1.call-start
  6.5 1.2 copy-done
  7.8 6.5 %fusion.13 = (f32[2,1056]{1,0:T(2,128)S(1)}, f32[2,64,1056]{2,1,0:T(8,128)S(1)}) fusion(bf16[2,64,4224]{2,1,0:T(8,128)(2,1)S(1)} %copy-done, bf16[4224,1056]{0,1:T(8,128)(2,1)} %param.3), kind=kOutput, calls=%fused_computation.25 | convolution fusion | flops 1142032384 | bytes 10551552 | tf_op jit(solution)/shard_map/vbh,hc->vbc/dot_general | solution.py:16
  14.3 15.7 %psum.14 = f32[2,1,1056]{2,0,1:T(2,128)S(1)} all-reduce(f32[2,1,1056]{2,0,1:T(2,128)S(1)} %bitcast.30), channel_id=1, replica_groups=mesh['dp'=8,'mp'=4] {'dp'}, use_global_device_ids=true, to_apply=%region_1.0 | all-reduce | flops 2112 | bytes 16896 | tf_op jit(solution)/shard_map/psum | solution.py:17
  30.0 0.1 multiply_reduce_fusion
  30.1 12.4 %psum.15 = f32[2,1,1056]{2,0,1:T(2,128)S(1)} all-reduce(f32[2,1,1056]{2,0,1:T(2,128)S(1)} %bitcast.31), channel_id=1, replica_groups=mesh['dp'=8,'mp'=4] {'dp'}, use_global_device_ids=true, to_apply=%region_3.0 | all-reduce | flops 2112 | bytes 16896 | tf_op jit(solution)/shard_map/psum | solution.py:20
  42.5 0.6 add_sqrt_fusion
  43.1 0.1 divide_convert_fusion
  43.2 0.7 fusion.12
  43.9 0.0 all-gather.7.cloned.1.call-update
  43.9 1.2 copy.10
  45.1 39.8 %all-gather = bf16[1,64,4224]{1,0,2:T(2,128)(2,1)S(1)} all-gather(bf16[1,64,1056]{1,0,2:T(2,128)(2,1)} %copy.10), channel_id=2, replica_groups=mesh['dp'=8,'mp'=4] {'mp'}, dimensions={2}, use_global_device_ids=true | all-gather | bytes 675840 | tf_op jit(solution)/shard_map/all_gather | solution.py:25
  84.9 1.2 copy.16
  86.1 2.2 %copy.13 = bf16[64,8,528]{2,0,1:T(8,128)(2,1)} copy(bf16[64,8,528]{0,2,1:T(8,128)(2,1)} %bitcast.29) | data formatting | bytes 1081344 | tf_op jit(solution)/shard_map/all_to_all | solution.py:27
  88.3 4.2 %all-to-all-start = ((bf16[64,8,528]{2,0,1:T(8,128)(2,1)}), bf16[64,8,528]{2,0,1:T(8,128)(2,1)}, u32[]{:S(2)}, u32[]{:S(2)}) async-start(bf16[64,8,528]{2,0,1:T(8,128)(2,1)} %copy.13), calls=%async_computation | async-start | bytes 1310720 | tf_op jit(solution)/shard_map/all_to_all | solution.py:27
  92.5 0.2 all-gather.5.cloned.1.call-start
  92.8 10.9 %all-to-all-done = bf16[64,8,528]{2,0,1:T(8,128)(2,1)} async-done(((bf16[64,8,528]{2,0,1:T(8,128)(2,1)}), bf16[64,8,528]{2,0,1:T(8,128)(2,1)}, u32[]{:S(2)}, u32[]{:S(2)}) %all-to-all-start) | async-done | bytes 540704 | tf_op jit(solution)/shard_map/all_to_all | solution.py:27
  103.7 0.0 all-gather.7.cloned.1.call-done
  103.7 3.6 %select_convert_fusion = bf16[1056,528]{0,1:T(8,128)(2,1)} fusion(s32[1056]{0:T(1024)S(1)} %iota_add_fusion, s32[528]{0:T(1024)S(1)} %iota_add_fusion.1, bf16[512,528]{1,0:T(8,128)(2,1)} %bitcast.8, bf16[1,512,1056]{2,1,0:T(8,128)(2,1)} %all-gather.7.cloned.1.call-done), kind=kOutput, calls=%fused_computation.7 | convolution fusion | flops 574852608 | bytes 2743488 | tf_op jit(solution)/shard_map/bi,bj->ij/dot_general | solution.py:29
  107.3 0.0 all-gather.5.cloned.1.call-update
  107.3 3.7 %copy.11 = bf16[1,64,4224]{2,1,0:T(8,128)(2,1)} copy(bf16[1,64,4224]{1,0,2:T(2,128)(2,1)S(1)} %all-gather) | data formatting | bytes 1081344 | tf_op jit(solution)/shard_map/all_gather | solution.py:25
  110.9 0.7 divide_reduce_fusion
  111.7 55.5 %all-gather.5.cloned.1.call-done = bf16[1056,4224]{0,1:T(8,128)(2,1)} async-done(((bf16[1056,528]{0,1:T(8,128)(2,1)}), bf16[1056,4224]{0,1:T(8,128)(2,1)}) %all-gather.5.cloned.1.call-update) | async-done | bytes 8921104 | tf_op jit(solution)/shard_map/all_gather | solution.py:42
  167.2 0.0 copy-start.1
  167.2 10.4 %fusion = (f32[1056]{0:T(1024)S(1)}, f32[1056]{0:T(1024)S(1)}) fusion(bf16[1056,4224]{0,1:T(8,128)(2,1)} %all-gather.5.cloned.1.call-done, s32[1056]{0:T(1024)S(1)} %iota_add_fusion), kind=kLoop, calls=%fused_computation.2 | loop fusion | flops 26761152 | bytes 8933760 | tf_op jit(solution)/shard_map/reduce_sum | solution.py:46
  177.6 0.0 copy-done.1
  177.6 3.5 %fusion.5 = bf16[64,1056]{1,0:T(8,128)(2,1)} fusion(bf16[1056,4224]{0,1:T(8,128)(2,1)S(1)} %copy-done.1, bf16[1,64,4224]{2,1,0:T(8,128)(2,1)} %copy.11, f32[1056]{0:T(1024)S(1)} %divide_reduce_fusion, f32[1056]{0:T(1024)S(1)} %multiply_add_fusion, bf16[2,64,1056]{2,1,0:T(8,128)(2,1)S(1)} %divide_convert_fusion), kind=kOutput, calls=%fused_computation.10 | convolution fusion | flops 571287552 | bytes 9740544 | tf_op jit(solution)/shard_map/bj,ij->bi/dot_general | solution.py:49
  (4 shorter events, 0.0 us)
Async XLA Ops:
  6.5 1.2 copy-start
  6.5 97.1 %all-gather.7.cloned.1.call-start = ((), (), s32[]{:S(2)}) async-start(), calls=%async_computation.2 | async-start | bytes 1327104 | tf_op jit(solution)/shard_map/all_gather | solution.py:31
  88.3 15.4 %all-to-all-start = ((bf16[64,8,528]{2,0,1:T(8,128)(2,1)}), bf16[64,8,528]{2,0,1:T(8,128)(2,1)}, u32[]{:S(2)}, u32[]{:S(2)}) async-start(bf16[64,8,528]{2,0,1:T(8,128)(2,1)} %copy.13), calls=%async_computation | async-start | bytes 1310720 | tf_op jit(solution)/shard_map/all_to_all | solution.py:27
  92.5 74.6 %all-gather.5.cloned.1.call-start = ((), (), s32[]{:S(2)}) async-start(), calls=%async_computation.1 | async-start | bytes 10948608 | tf_op jit(solution)/shard_map/all_gather | solution.py:42
  167.2 10.4 %copy-start.1 = (bf16[1056,4224]{0,1:T(8,128)(2,1)S(1)}, bf16[1056,4224]{0,1:T(8,128)(2,1)}, u32[]{:S(2)}) copy-start(bf16[1056,4224]{0,1:T(8,128)(2,1)} %all-gather.5.cloned.1.call-done) | copy-start | bytes 26763268
Sparse Core Ops, SparseCore 0:
  44.0 23.4 all-gather.6
  107.4 59.7 all-gather.4
where the time goes:
time: 188 us
  blocking collectives  67.9 us (36%)
  waiting for transfers between devices  66.4 us (35%)
  matrix products  13.6 us (7%)
  between operations  13.5 us (7%)
  other arithmetic  11.9 us (6%)
  local copies, waits for them, and re-layouts  10.2 us (5%)
  starting transfers between devices  4.43 us (2%)
    all_gather x1, waiting for transfers between devices, shards(): grad_rows = lax.all_gather(grad_block, 'dp', axis=1, tiled=True)  55.5 us
    all_gather x1, blocking collectives, shards(): second_full = lax.all_gather(second, 'mp', axis=1, tiled=True)  39.8 us
    psum x1, blocking collectives, shards(): sums = lax.psum(jnp.sum(feats, axis=1, keepdims=True), 'dp')  15.7 us
    psum x1, blocking collectives, shards(): lax.psum(jnp.sum(centered * centered, axis=1, keepdims=True), 'dp') / total  12.4 us
    all_to_all x1, waiting for transfers between devices, shards(): lax.all_to_all(second_full, 'dp', split_axis=1, concat_axis=0, tiled=True)  10.9 us
    reduce_sum x1, other arithmetic, shards(): jnp.sum(grad_wide * grad_wide, axis=1) - diag_val * diag_val  10.4 us
    dot_general x1, matrix products, shards(): jnp.einsum('vbh,hc->vbc', hidden, proj_weight, preferred_element_type=jnp...  6.54 us
    all_to_all x1, starting transfers between devices, shards(): lax.all_to_all(second_full, 'dp', split_axis=1, concat_axis=0, tiled=True)  4.2 us
  transfers between devices with their start and end apart: 3, of which 2 were waited for; matrix products, arithmetic and copies ran while one was open for 5% of the time, Pallas kernels for 0%

commit v1 on v0

v1 whole, which is shorter than its diff:
```python
import functools

import jax
import jax.numpy as jnp
from jax import lax
from jax.experimental import pallas as pl
from jax.experimental.pallas import tpu as pltpu
from jax.sharding import PartitionSpec as P

off_weight = 0.0051
eps = 1e-05
CW = 384
MESH = pl.DeviceIdType.MESH
F32 = jnp.float32
BF16 = jnp.bfloat16


def kernel(
    D, Z, n_chunk, cols, h_ref, w_ref, o_ref,
    own, blk, nrm, stats, mom, kpart, ksend, krecv, msum, qsend, qrecv,
    s_send, s_recv, s_fwd, s_frecv, t_send, t_recv, t_fwd, t_frecv,
    k_send, k_recv, q_send, q_recv,
):
    C = D // 2
    R = h_ref.shape[1]
    B = R * D
    step = pl.program_id(0)
    dp = lax.axis_index("dp")
    mp = lax.axis_index("mp")
    chip = dp // 2
    core = lax.rem(dp, 2)
    sib = chip * 2 + (1 - core)

    def peer_chip(k):
        return lax.rem(chip + k, C)

    def dev(c, k):
        return c * 2 + k

    def block_copy(v, j, k):
        return pltpu.make_async_remote_copy(
            src_ref=blk.at[v, j, dp], dst_ref=blk.at[v, j, dp],
            send_sem=s_send.at[v, j, k], recv_sem=s_recv.at[v, j, C - k],
            device_id=(dev(peer_chip(k), core), mp), device_id_type=MESH)

    def block_fwd(v, j, k):
        src = dev(peer_chip(k), core)
        return pltpu.make_async_remote_copy(
            src_ref=blk.at[v, j, src], dst_ref=blk.at[v, j, src],
            send_sem=s_fwd.at[v, j, k], recv_sem=s_frecv.at[v, j, k],
            device_id=(sib, mp), device_id_type=MESH)

    def block_in(v, j, k):
        src = dev(peer_chip(k), core)
        return pltpu.make_async_remote_copy(
            src_ref=blk.at[v, j, src], dst_ref=blk.at[v, j, src],
            send_sem=s_send.at[v, j, k], recv_sem=s_recv.at[v, j, k],
            device_id=(sib, mp), device_id_type=MESH)

    def block_fin(v, j, k):
        src = dev(peer_chip(k), 1 - core)
        return pltpu.make_async_remote_copy(
            src_ref=blk.at[v, j, src], dst_ref=blk.at[v, j, src],
            send_sem=s_fwd.at[v, j, k], recv_sem=s_frecv.at[v, j, k],
            device_id=(sib, mp), device_id_type=MESH)

    def stat_copy(k):
        return pltpu.make_async_remote_copy(
            src_ref=stats.at[dp], dst_ref=stats.at[dp],
            send_sem=t_send.at[k], recv_sem=t_recv.at[D - k],
            device_id=(lax.rem(dp + k, D), mp), device_id_type=MESH)

    def stat_in(k):
        src = lax.rem(dp + k, D)
        return pltpu.make_async_remote_copy(
            src_ref=stats.at[src], dst_ref=stats.at[src],
            send_sem=t_send.at[k], recv_sem=t_recv.at[k],
            device_id=(src, mp), device_id_type=MESH)

    def k_copy(k):
        return pltpu.make_async_remote_copy(
            src_ref=ksend, dst_ref=krecv.at[Z - k],
            send_sem=k_send.at[k], recv_sem=k_recv.at[Z - k],
            device_id=(dp, lax.rem(mp + k, Z)), device_id_type=MESH)

    def k_in(k):
        return pltpu.make_async_remote_copy(
            src_ref=ksend, dst_ref=krecv.at[k],
            send_sem=k_send.at[k], recv_sem=k_recv.at[k],
            device_id=(dp, lax.rem(mp + k, Z)), device_id_type=MESH)

    def q_copy(k):
        return pltpu.make_async_remote_copy(
            src_ref=qsend, dst_ref=qrecv.at[D - k],
            send_sem=q_send.at[k], recv_sem=q_recv.at[D - k],
            device_id=(lax.rem(dp + k, D), mp), device_id_type=MESH)

    def q_in(k):
        return pltpu.make_async_remote_copy(
            src_ref=qsend, dst_ref=qrecv.at[k],
            send_sem=q_send.at[k], recv_sem=q_recv.at[k],
            device_id=(lax.rem(dp + k, D), mp), device_id_type=MESH)

    def each(lo, hi, f):
        def body(k, _):
            f(k)
            return 0
        lax.fori_loop(lo, hi, body, 0)

    barrier = pltpu.get_barrier_semaphore()

    @pl.when(step == 0)
    def _():
        each(1, D, lambda k: pl.semaphore_signal(
            barrier, inc=1, device_id=(lax.rem(dp + k, D), mp), device_id_type=MESH))
        each(1, Z, lambda k: pl.semaphore_signal(
            barrier, inc=1, device_id=(dp, lax.rem(mp + k, Z)), device_id_type=MESH))

    f = jnp.dot(h_ref[...].reshape(2 * R, h_ref.shape[2]), w_ref[...], preferred_element_type=F32)
    lane = step * CW + lax.broadcasted_iota(jnp.int32, (1, CW), 1)
    f = jnp.where(lane < cols, f, 0.0)
    for v in range(2):
        fv = f[v * R:(v + 1) * R]
        mean = jnp.sum(fv, axis=0, keepdims=True) / R
        c = fv - mean
        m2 = jnp.sum(c * c, axis=0, keepdims=True)
        own[v, step] = c
        blk[v, step, dp] = c.astype(BF16)
        stats[dp, 2 * v, step] = mean[0]
        stats[dp, 2 * v + 1, step] = m2[0]

    @pl.when(step == 0)
    def _():
        pl.semaphore_wait(barrier, D - 1 + Z - 1)

    def send(v, j):
        each(1, C, lambda k: block_copy(v, j, k).start())
        block_fwd(v, j, 0).start()

    send(1, step)

    @pl.when(step == n_chunk - 1)
    def _():
        each(1, D, lambda k: stat_copy(k).start())
        for j in range(n_chunk):
            send(0, j)

        def forward(v):
            for j in range(n_chunk):
                def go(k, j=j):
                    block_in(v, j, k).wait_recv()
                    block_fwd(v, j, k).start()
                each(1, C, go)

        def moments(v, j):
            mean = jnp.mean(stats[:, 2 * v, j], axis=0, keepdims=True)
            dev_mean = stats[:, 2 * v, j] - mean
            var = (jnp.sum(stats[:, 2 * v + 1, j], axis=0, keepdims=True)
                   + R * jnp.sum(dev_mean * dev_mean, axis=0, keepdims=True)) / B
            return mean, var

        def normalize(v):
            for j in range(n_chunk):
                each(0, C, lambda k, j=j: block_fin(v, j, k).wait_recv())
            for j in range(n_chunk):
                mean, var = moments(v, j)
                inv = 1.0 / jnp.sqrt(var + eps)
                mom[v, j, 0] = mean[0]
                mom[v, j, 1] = inv[0]

                def go(d, j=j, mean=mean, inv=inv, v=v):
                    shift = stats[d, pl.ds(2 * v, 1), j] - mean
                    nrm[v, j, d] = ((blk[v, j, d].astype(F32) + shift) * inv).astype(BF16)
                each(0, D, go)

        forward(1)
        each(1, D, lambda k: stat_in(k).wait_recv())
        normalize(1)

        G = 4
        def kgroup(g):
            acc = jnp.zeros((R, G * R), F32)
            for j in range(n_chunk):
                mine = nrm[1, j, dp]
                rest = nrm[1, j, pl.ds(g * G, G)].reshape(G * R, CW)
                acc += lax.dot_general(mine, rest, (((1,), (1,)), ((), ())),
                                       preferred_element_type=F32)
            at = pl.ds(pl.multiple_of(g * (G * R), G * R), G * R)
            kpart[:, at] = acc
            ksend[:, at] = acc.astype(BF16)
        each(0, D // G, kgroup)
        each(1, Z, lambda k: k_copy(k).start())

        forward(0)
        normalize(0)

        for j in range(n_chunk):
            def dsum(d, t, j=j):
                return t + nrm[0, j, d].astype(F32) * nrm[1, j, d].astype(F32)
            t = lax.fori_loop(0, D, dsum, jnp.zeros((R, CW), F32))
            mom[0, j, 2] = jnp.sum(t, axis=0) / B

        each(1, Z, lambda k: k_in(k).wait_recv())
        kb = lax.fori_loop(1, Z, lambda k, t: t + krecv[k].astype(F32), kpart[...]).astype(BF16)
        for j in range(n_chunk):
            m = jnp.dot(kb, nrm[0, j].reshape(B, CW), preferred_element_type=F32)
            msum[j] = m
            qsend[0, j] = jnp.sum(m * nrm[0, j, dp].astype(F32), axis=0)
        each(1, D, lambda k: q_copy(k).start())

        def own_norm(v, j):
            mean = mom[v, j, pl.ds(0, 1)]
            inv = mom[v, j, pl.ds(1, 1)]
            shift = stats[dp, pl.ds(2 * v, 1), j] - mean
            return ((own[v, j] + shift) * inv).astype(BF16).astype(F32)

        each(1, D, lambda k: q_in(k).wait_recv())
        for j in range(n_chunk):
            w = min(CW, cols - j * CW)
            q = lax.fori_loop(1, D, lambda k, t, j=j: t + qrecv[k, :, j],
                              qsend[:, j]) / (float(B) * B)
            cd = mom[0, j, pl.ds(2, 1)]
            inv = mom[0, j, pl.ds(1, 1)]
            g = (2.0 * (cd - 1.0)).astype(BF16).astype(F32)
            scale = 2.0 * off_weight * (q - cd * cd) + g * (1.0 + g / 2.0)
            res = ((2.0 * off_weight / B) * msum[j]
                   + own_norm(1, j) * (g - 2.0 * off_weight * cd)
                   - own_norm(0, j) * scale) * inv
            o_ref[:, j * CW:j * CW + w] = res[:, :w].astype(BF16)

        for v in range(2):
            for j in range(n_chunk):
                each(1, C, lambda k, v=v, j=j: block_copy(v, j, k).wait_send())
                each(0, C, lambda k, v=v, j=j: block_fwd(v, j, k).wait_send())
        each(1, D, lambda k: stat_copy(k).wait_send())
        each(1, Z, lambda k: k_copy(k).wait_send())
        each(1, D, lambda k: q_copy(k).wait_send())


def shards(D, Z, hidden, w):
    _, R, H = hidden.shape
    cols = w.shape[1]
    n = pl.cdiv(cols, CW)
    B = R * D
    dma = pltpu.SemaphoreType.DMA
    C = D // 2
    return pl.pallas_call(
        functools.partial(kernel, D, Z, n, cols),
        grid=(n,),
        out_shape=jax.ShapeDtypeStruct((R, cols), BF16),
        in_specs=[
            pl.BlockSpec((2, R, H), lambda i: (0, 0, 0)),
            pl.BlockSpec((H, CW), lambda i: (0, i)),
        ],
        out_specs=pl.BlockSpec((R, cols), lambda i: (0, 0)),
        scratch_shapes=[
            pltpu.VMEM((2, n, R, CW), F32),
            pltpu.VMEM((2, n, D, R, CW), BF16),
            pltpu.VMEM((2, n, D, R, CW), BF16),
            pltpu.VMEM((D, 4, n, CW), F32),
            pltpu.VMEM((2, n, 4, CW), F32),
            pltpu.VMEM((R, B), F32),
            pltpu.VMEM((R, B), BF16),
            pltpu.VMEM((Z, R, B), BF16),
            pltpu.VMEM((n, R, CW), F32),
            pltpu.VMEM((1, n, CW), F32),
            pltpu.VMEM((D, 1, n, CW), F32),
            dma((2, n, C)), dma((2, n, C)), dma((2, n, C)), dma((2, n, C)),
            dma((D,)), dma((D,)), dma((D,)), dma((D,)),
            dma((Z,)), dma((Z,)),
            dma((D,)), dma((D,)),
        ],
        compiler_params=pltpu.CompilerParams(
            collective_id=0, has_side_effects=True, vmem_limit_bytes=56 * 2**20,
            dimension_semantics=("arbitrary",)),
        cost_estimate=pl.CostEstimate(
            flops=4 * R * H * cols, bytes_accessed=2 * H * cols, transcendentals=0),
    )(hidden, w)


def solution(mesh):
    D, Z = mesh.shape["dp"], mesh.shape["mp"]
    return jax.shard_map(
        functools.partial(shards, D, Z),
        mesh=mesh,
        in_specs=(P(None, "dp", None), P(None, "mp")),
        out_specs=P("dp", "mp"),
        check_vma=False,
    )
```

time: 188 us -> 48.4 us (0.26)
  blocking collectives: 67.9 us -> 0 us
  waiting for transfers between devices: 66.4 us -> 0 us
  Pallas kernels: 0 us -> 32.7 us
  matrix products: 13.6 us -> 0 us
  between operations: 13.5 us -> 0.01 us
  other arithmetic: 11.9 us -> 0 us
  local copies, waits for them, and re-layouts: 10.2 us -> 15.3 us
  starting transfers between devices: 4.43 us -> 0 us
    all_gather x2 -> x0, waiting for transfers between devices: 55.5 us -> none  [the longest x1 55.5 us: shards(): grad_rows = lax.all_gather(grad_block, 'dp', axis=1, tiled=True)]
    all_gather x1 -> x0, blocking collectives: 39.8 us -> none  [shards(): second_full = lax.all_gather(second, 'mp', axis=1, tiled=True)]
    pallas_call x0 -> x1, Pallas kernels: none -> 32.7 us  [shards(): pl.pallas_call(functools.partial(kernel, D, Z, n, cols), grid=(n,), out_s...]
    psum x2 -> x0, blocking collectives: 28.1 us -> none  [the longest x1 15.7 us: shards(): sums = lax.psum(jnp.sum(feats, axis=1, keepdims=True), 'dp')]
    dot_general x3 -> x0, matrix products: 13.6 us -> none  [the longest x1 6.54 us: shards(): jnp.einsum('vbh,hc->vbc', hidden, proj_weight, preferred_element_type=jnp...]
    unnamed x5 -> x2, local copies, waits for them, and re-layouts: 2.41 us -> 15.3 us
    all_to_all x1 -> x0, waiting for transfers between devices: 10.9 us -> none  [shards(): lax.all_to_all(second_full, 'dp', split_axis=1, concat_axis=0, tiled=True)]
    reduce_sum x2 -> x0, other arithmetic: 10.5 us -> none  [the longest x1 10.4 us: shards(): jnp.sum(grad_wide * grad_wide, axis=1) - diag_val * diag_val]
  transfers between devices with their start and end apart: 3 -> 0, of which waited for: 2 -> 0; matrix products, arithmetic and copies ran while one was open for 5% -> 0% of each run, Pallas kernels for 0% -> 0%
where the time goes in v1:
time: 48.4 us; the launch traced here: 48 us
  Pallas kernels  32.7 us (68%)
  local copies, waits for them, and re-layouts  15.3 us (32%)
    pallas_call x1, Pallas kernels, shards(): pl.pallas_call(functools.partial(kernel, D, Z, n, cols), grid=(n,), out_s...  32.7 us
    unnamed x2, local copies, waits for them, and re-layouts  15.3 us

profile of v1, /device:TPU:0, one launch (start us, length us, event | category | flops | bytes accessed | tf_op | source)
XLA Modules:
  0.0 48.0 jit_solution(15319051550363776017)
XLA Ops:
  0.0 13.7 %copy.3.w_ref = bf16[4224,1056]{1,0:T(8,128)(2,1)} copy(bf16[4224,1056]{0,1:T(8,128)(2,1)} %param.3) | data formatting | bytes 17842176 | tf_op args[1]
  13.7 32.7 %shard_map.28 = bf16[64,1056]{1,0:T(8,128)(2,1)} custom-call(bf16[2,64,4224]{2,1,0:T(8,128)(2,1)} %h_ref.1, bf16[4224,1056]{1,0:T(8,128)(2,1)} %copy.3.w_ref), custom_call_target="tpu_custom_call" | custom-call | flops 1141899264 | bytes 8921088 | tf_op jit(solution)/shard_map/pallas_call | solution.py:247
  46.4 1.6 %copy.5 = bf16[64,1056]{1,0:T(8,128)(2,1)} copy(bf16[64,1056]{1,0:T(8,128)(2,1)} %shard_map.28) | data formatting | bytes 270336

commit v2 on v1

v2 whole, which is shorter than its diff:
```python
import functools

import jax
import jax.numpy as jnp
from jax import lax
from jax.experimental import pallas as pl
from jax.experimental.pallas import tpu as pltpu
from jax.sharding import PartitionSpec as P

off_weight = 0.0051
eps = 1e-05
CW = 384
MESH = pl.DeviceIdType.MESH
F32 = jnp.float32
BF16 = jnp.bfloat16


def kernel(
    D, Z, n_chunk, cols, h_hbm, w_hbm, o_ref,
    h_ref, w_ref, own, blk, nrm, stats, mom, kpart, ksend, krecv, msum, qsend, qrecv,
    s_send, s_recv, s_fwd, s_frecv, t_send, t_recv, t_fwd, t_frecv,
    k_send, k_recv, q_send, q_recv, h_sem, w_sem,
):
    C = D // 2
    R = h_hbm.shape[1]
    B = R * D
    dp = lax.axis_index("dp")
    mp = lax.axis_index("mp")
    chip = dp // 2
    core = lax.rem(dp, 2)
    sib = chip * 2 + (1 - core)

    def peer_chip(k):
        return lax.rem(chip + k, C)

    def dev(c, k):
        return c * 2 + k

    def block_copy(v, j, k):
        return pltpu.make_async_remote_copy(
            src_ref=blk.at[v, dp, j], dst_ref=blk.at[v, dp, j],
            send_sem=s_send.at[v, j, k], recv_sem=s_recv.at[v, j, C - k],
            device_id=(dev(peer_chip(k), core), mp), device_id_type=MESH)

    def block_fwd(v, j, k):
        src = dev(peer_chip(k), core)
        return pltpu.make_async_remote_copy(
            src_ref=blk.at[v, src, j], dst_ref=blk.at[v, src, j],
            send_sem=s_fwd.at[v, j, k], recv_sem=s_frecv.at[v, j, k],
            device_id=(sib, mp), device_id_type=MESH)

    def block_in(v, j, k):
        src = dev(peer_chip(k), core)
        return pltpu.make_async_remote_copy(
            src_ref=blk.at[v, src, j], dst_ref=blk.at[v, src, j],
            send_sem=s_send.at[v, j, k], recv_sem=s_recv.at[v, j, k],
            device_id=(sib, mp), device_id_type=MESH)

    def block_fin(v, j, k):
        src = dev(peer_chip(k), 1 - core)
        return pltpu.make_async_remote_copy(
            src_ref=blk.at[v, src, j], dst_ref=blk.at[v, src, j],
            send_sem=s_fwd.at[v, j, k], recv_sem=s_frecv.at[v, j, k],
            device_id=(sib, mp), device_id_type=MESH)

    def stat_copy(k):
        return pltpu.make_async_remote_copy(
            src_ref=stats.at[dp], dst_ref=stats.at[dp],
            send_sem=t_send.at[k], recv_sem=t_recv.at[D - k],
            device_id=(lax.rem(dp + k, D), mp), device_id_type=MESH)

    def stat_in(k):
        src = lax.rem(dp + k, D)
        return pltpu.make_async_remote_copy(
            src_ref=stats.at[src], dst_ref=stats.at[src],
            send_sem=t_send.at[k], recv_sem=t_recv.at[k],
            device_id=(src, mp), device_id_type=MESH)

    def k_copy(k):
        return pltpu.make_async_remote_copy(
            src_ref=ksend, dst_ref=krecv.at[Z - k],
            send_sem=k_send.at[k], recv_sem=k_recv.at[Z - k],
            device_id=(dp, lax.rem(mp + k, Z)), device_id_type=MESH)

    def k_in(k):
        return pltpu.make_async_remote_copy(
            src_ref=ksend, dst_ref=krecv.at[k],
            send_sem=k_send.at[k], recv_sem=k_recv.at[k],
            device_id=(dp, lax.rem(mp + k, Z)), device_id_type=MESH)

    def q_copy(k):
        return pltpu.make_async_remote_copy(
            src_ref=qsend, dst_ref=qrecv.at[D - k],
            send_sem=q_send.at[k], recv_sem=q_recv.at[D - k],
            device_id=(lax.rem(dp + k, D), mp), device_id_type=MESH)

    def q_in(k):
        return pltpu.make_async_remote_copy(
            src_ref=qsend, dst_ref=qrecv.at[k],
            send_sem=q_send.at[k], recv_sem=q_recv.at[k],
            device_id=(lax.rem(dp + k, D), mp), device_id_type=MESH)

    def each(lo, hi, f):
        def body(k, _):
            f(k)
            return 0
        lax.fori_loop(lo, hi, body, 0)

    barrier = pltpu.get_barrier_semaphore()

    each(1, D, lambda k: pl.semaphore_signal(
        barrier, inc=1, device_id=(lax.rem(dp + k, D), mp), device_id_type=MESH))
    each(1, Z, lambda k: pl.semaphore_signal(
        barrier, inc=1, device_id=(dp, lax.rem(mp + k, Z)), device_id_type=MESH))

    h_load = pltpu.make_async_copy(h_hbm, h_ref, h_sem)
    h_load.start()
    w_loads = []
    for j in range(n_chunk):
        at = pl.ds(j * CW, min(CW, cols - j * CW))
        w_loads.append(pltpu.make_async_copy(w_hbm.at[at], w_ref.at[at], w_sem.at[j]))
        w_loads[j].start()
    h_load.wait()

    def send(v, j):
        each(1, C, lambda k: block_copy(v, j, k).start())
        block_fwd(v, j, 0).start()

    for j in range(n_chunk):
        w_loads[j].wait()
        f = lax.dot_general(h_ref[...].reshape(2 * R, h_ref.shape[2]), w_ref[pl.ds(j * CW, CW)],
                            (((1,), (1,)), ((), ())), preferred_element_type=F32)
        lane = j * CW + lax.broadcasted_iota(jnp.int32, (1, CW), 1)
        f = jnp.where(lane < cols, f, 0.0)
        for v in range(2):
            fv = f[v * R:(v + 1) * R]
            mean = jnp.sum(fv, axis=0, keepdims=True) / R
            c = fv - mean
            m2 = jnp.sum(c * c, axis=0, keepdims=True)
            own[v, j] = c
            blk[v, dp, j] = c.astype(BF16)
            stats[dp, 2 * v, j] = mean[0]
            stats[dp, 2 * v + 1, j] = m2[0]
        if j == 0:
            pl.semaphore_wait(barrier, D - 1 + Z - 1)
        send(1, j)

    each(1, D, lambda k: stat_copy(k).start())
    for j in range(n_chunk):
        send(0, j)

    def forward(v):
        for j in range(n_chunk):
            def go(k, j=j):
                block_in(v, j, k).wait_recv()
                block_fwd(v, j, k).start()
            each(1, C, go)

    def moments(v, j):
        mean = jnp.mean(stats[:, 2 * v, j], axis=0, keepdims=True)
        dev_mean = stats[:, 2 * v, j] - mean
        var = (jnp.sum(stats[:, 2 * v + 1, j], axis=0, keepdims=True)
               + R * jnp.sum(dev_mean * dev_mean, axis=0, keepdims=True)) / B
        return mean, var

    def normalize(v):
        scales = []
        for j in range(n_chunk):
            mean, var = moments(v, j)
            inv = 1.0 / jnp.sqrt(var + eps)
            mom[v, j, 0] = mean[0]
            mom[v, j, 1] = inv[0]
            scales.append((mean, inv))

        def one(d):
            for j in range(n_chunk):
                mean, inv = scales[j]
                shift = stats[d, pl.ds(2 * v, 1), j] - mean
                nrm[v, j, d] = ((blk[v, d, j].astype(F32) + shift) * inv).astype(BF16)

        each(0, C, lambda k: one(dev(peer_chip(k), core)))
        def late(k):
            for j in range(n_chunk):
                block_fin(v, j, k).wait_recv()
            one(dev(peer_chip(k), 1 - core))
        each(0, C, late)

    forward(1)
    each(1, D, lambda k: stat_in(k).wait_recv())
    normalize(1)

    G = 4
    def kgroup(g):
        acc = jnp.zeros((R, G * R), F32)
        for j in range(n_chunk):
            mine = nrm[1, j, dp]
            rest = nrm[1, j, pl.ds(g * G, G)].reshape(G * R, CW)
            acc += lax.dot_general(mine, rest, (((1,), (1,)), ((), ())),
                                   preferred_element_type=F32)
        at = pl.ds(pl.multiple_of(g * (G * R), G * R), G * R)
        kpart[:, at] = acc
        ksend[:, at] = acc.astype(BF16)
    each(0, D // G, kgroup)
    each(1, Z, lambda k: k_copy(k).start())

    forward(0)
    normalize(0)

    for j in range(n_chunk):
        def dsum(d, t, j=j):
            return t + nrm[0, j, d].astype(F32) * nrm[1, j, d].astype(F32)
        t = lax.fori_loop(0, D, dsum, jnp.zeros((R, CW), F32))
        mom[0, j, 2] = jnp.sum(t, axis=0) / B

    each(1, Z, lambda k: k_in(k).wait_recv())
    kb = lax.fori_loop(1, Z, lambda k, t: t + krecv[k].astype(F32), kpart[...]).astype(BF16)
    for j in range(n_chunk):
        m = jnp.dot(kb, nrm[0, j].reshape(B, CW), preferred_element_type=F32)
        msum[j] = m
        qsend[0, j] = jnp.sum(m * nrm[0, j, dp].astype(F32), axis=0)
    each(1, D, lambda k: q_copy(k).start())

    def own_norm(v, j):
        mean = mom[v, j, pl.ds(0, 1)]
        inv = mom[v, j, pl.ds(1, 1)]
        shift = stats[dp, pl.ds(2 * v, 1), j] - mean
        return ((own[v, j] + shift) * inv).astype(BF16).astype(F32)

    each(1, D, lambda k: q_in(k).wait_recv())
    for j in range(n_chunk):
        w = min(CW, cols - j * CW)
        q = lax.fori_loop(1, D, lambda k, t, j=j: t + qrecv[k, :, j],
                          qsend[:, j]) / (float(B) * B)
        cd = mom[0, j, pl.ds(2, 1)]
        inv = mom[0, j, pl.ds(1, 1)]
        g = (2.0 * (cd - 1.0)).astype(BF16).astype(F32)
        scale = 2.0 * off_weight * (q - cd * cd) + g * (1.0 + g / 2.0)
        res = ((2.0 * off_weight / B) * msum[j]
               + own_norm(1, j) * (g - 2.0 * off_weight * cd)
               - own_norm(0, j) * scale) * inv
        o_ref[:, j * CW:j * CW + w] = res[:, :w].astype(BF16)

    for v in range(2):
        for j in range(n_chunk):
            each(1, C, lambda k: block_copy(v, j, k).wait_send())
            each(0, C, lambda k: block_fwd(v, j, k).wait_send())
    each(1, D, lambda k: stat_copy(k).wait_send())
    each(1, Z, lambda k: k_copy(k).wait_send())
    each(1, D, lambda k: q_copy(k).wait_send())


def shards(D, Z, hidden, w):
    _, R, H = hidden.shape
    cols = w.shape[1]
    n = pl.cdiv(cols, CW)
    B = R * D
    dma = pltpu.SemaphoreType.DMA
    C = D // 2
    return pl.pallas_call(
        functools.partial(kernel, D, Z, n, cols),
        out_shape=jax.ShapeDtypeStruct((R, cols), BF16),
        in_specs=[
            pl.BlockSpec(memory_space=pl.ANY),
            pl.BlockSpec(memory_space=pl.ANY),
        ],
        out_specs=pl.BlockSpec(memory_space=pltpu.VMEM),
        scratch_shapes=[
            pltpu.VMEM((2, R, H), BF16),
            pltpu.VMEM((n * CW, H), BF16),
            pltpu.VMEM((2, n, R, CW), F32),
            pltpu.VMEM((2, D, n, R, CW), BF16),
            pltpu.VMEM((2, n, D, R, CW), BF16),
            pltpu.VMEM((D, 4, n, CW), F32),
            pltpu.VMEM((2, n, 4, CW), F32),
            pltpu.VMEM((R, B), F32),
            pltpu.VMEM((R, B), BF16),
            pltpu.VMEM((Z, R, B), BF16),
            pltpu.VMEM((n, R, CW), F32),
            pltpu.VMEM((1, n, CW), F32),
            pltpu.VMEM((D, 1, n, CW), F32),
            dma((2, n, C)), dma((2, n, C)), dma((2, n, C)), dma((2, n, C)),
            dma((D,)), dma((D,)), dma((D,)), dma((D,)),
            dma((Z,)), dma((Z,)),
            dma((D,)), dma((D,)),
            dma, dma((n,)),
        ],
        compiler_params=pltpu.CompilerParams(
            collective_id=0, has_side_effects=True, vmem_limit_bytes=56 * 2**20),
        cost_estimate=pl.CostEstimate(
            flops=4 * R * H * cols, bytes_accessed=2 * H * cols, transcendentals=0),
    )(hidden, w.T)


def solution(mesh):
    D, Z = mesh.shape["dp"], mesh.shape["mp"]
    return jax.shard_map(
        functools.partial(shards, D, Z),
        mesh=mesh,
        in_specs=(P(None, "dp", None), P(None, "mp")),
        out_specs=P("dp", "mp"),
        check_vma=False,
    )
```

time: 48.4 us -> 34.1 us (0.70)
  local copies, waits for them, and re-layouts: 15.3 us -> 1.58 us
    unnamed x2 -> x1, local copies, waits for them, and re-layouts: 15.3 us -> 1.58 us
where the time goes in v2:
time: 34.1 us; the launch traced here: 33.9 us
  Pallas kernels  32.3 us (95%)
  local copies, waits for them, and re-layouts  1.58 us (5%)
    pallas_call x1, Pallas kernels, shards(): pl.pallas_call(functools.partial(kernel, D, Z, n, cols), out_shape=jax.Sh...  32.3 us
    unnamed x1, local copies, waits for them, and re-layouts  1.58 us

profile of v2, /device:TPU:0, one launch (start us, length us, event | category | flops | bytes accessed | tf_op | source)
XLA Modules:
  0.0 33.9 jit_solution(5110599163603871440)
XLA Ops:
  0.0 32.3 %shard_map.28 = bf16[64,1056]{1,0:T(8,128)(2,1)} custom-call(bf16[2,64,4224]{2,1,0:T(8,128)(2,1)} %h_hbm.1, bf16[1056,4224]{1,0:T(8,128)(2,1)} %bitcast.1), custom_call_target="tpu_custom_call" | custom-call | flops 1141899264 | bytes 8921088 | tf_op jit(solution)/shard_map/pallas_call | solution.py:259
  32.3 1.6 %copy.4 = bf16[64,1056]{1,0:T(8,128)(2,1)} copy(bf16[64,1056]{1,0:T(8,128)(2,1)} %shard_map.28) | data formatting | bytes 270336
